TPU v7x, 128 devices: a whole 4x4x4 slice. The times are simulated.
128 devices in a mesh: ctx: 8 (over x, z_hi), grp: 16 (over y, z_lo, core).
Axes of the slice: x: 4, y: 4, z: 4 (z_hi: 2, z_lo: 2; z = z_hi * 2 + z_lo), core: 2. Of those that a mesh axis runs over, the one named last changes fastest.
Arguments:
- tail_q: bfloat16 [16, 512, 8192], P('grp', 'ctx'), may hold values from -6 to 6
- prompt_kv: bfloat16 [16, 4480, 2048], P('grp', 'ctx'), may hold values from -6 to 6
- dest_owner: int32 [16, 8, 35, 1], P('grp', 'ctx'), may hold values from 0 to 15; in each aligned block of 35 rows (0 to 34, 35 to 69, ..., all dimensions but the last counted through in order) at most 5 rows name the same one
- dest_row: int32 [16, 8, 35], P('grp', 'ctx'), may hold values from 0 to 3
- dec_q: bfloat16 [64, 2, 8192], P('grp'), may hold values from -6 to 6
- new_kv: bfloat16 [64, 2, 2048], P('grp'), may hold values from -6 to 6
- res_kv: bfloat16 [64, 1024, 2048], P('grp', 'ctx'), may hold values from -6 to 6
- lens: int32 [64], P('grp'), may hold values from 1 to 1024, 32768 in all
Outputs:
- prefill_out: bfloat16 [16, 512, 8192], P('grp', 'ctx')
- decode_out: bfloat16 [64, 2, 8192], P('grp', None, 'ctx')
Inputs may be any that keep to these rules, and one draw needn't show every extreme that they name: `dest_owner`: among the 35 blocks of one prompt shard (one device), no owner is named more than 5 times; in some shards one owner is named exactly 5 times.
All inputs are finite; a program needn't handle non-finite values. No bound on the sum of `lens` on one device may be relied on, other than what follows from the above.
Results may differ from a plain program's by a relative error of at most 0.012.
Values may be sent and summed in bfloat16 or wider, within the bound.
No kernel may reach another device: no remote copies, remote signals or barrier semaphores. Data moves between devices by JAX's collectives and lax.ppermute only.
A program may use at most 128 MiB of HBM per device.

v0:
```python
import math
import jax
import jax.numpy as jnp
from jax import lax
from jax.sharding import PartitionSpec as P

H = 64
KVH = 8
HD = 128
PRE_DEV = 496
TAIL_DEV = 64
BLK = 16
ROW_GRP = 4
RES_DEV = 128
GROUP = 8
KVD = 1024
QD = 8192
SEQ_DEV = 560
NB = 35
MASKED = -jnp.inf
FLOOR = -1e30


def merged(value, axis, join):
    pieces = jax.tree.map(lambda part: lax.all_gather(part, axis), value)
    head = jax.tree.map(lambda part: part[0], pieces)
    tail = jax.tree.map(lambda part: part[1:], pieces)
    subtotal, _ = lax.scan(lambda subtotal, share: (join(subtotal, share), None), head, tail)
    return subtotal


def key_allowed(key_index, query_pos):
    offset = key_index % SEQ_DEV
    tail_pos = jnp.where(offset >= PRE_DEV, key_index // SEQ_DEV * TAIL_DEV + offset - PRE_DEV, -1)
    return tail_pos[None, :] <= query_pos[:, None]


def join_parts(first_part, second_part):
    peak_first, total_first, mixed_first = first_part
    peak_second, total_second, mixed_second = second_part
    peak = jnp.maximum(peak_first, peak_second)
    fade_first = jnp.exp(peak_first - peak)
    fade_second = jnp.exp(peak_second - peak)
    total = total_first * fade_first + total_second * fade_second
    mixed = mixed_first * fade_first[..., None] + mixed_second * fade_second[..., None]
    return (peak, total, mixed)


def local(tail_q, prompt_kv, dest_owner, dest_row, dec_q, new_kv, res_kv, lens):
    scale = 1.0 / math.sqrt(HD)
    ctx_pos = lax.axis_index("ctx")
    n_ctx = lax.axis_size("ctx")
    n_grp = lax.axis_size("grp")
    per_owner = max(2, (2 * NB + n_grp - 1) // n_grp)
    own_pos = ctx_pos * TAIL_DEV + jnp.arange(TAIL_DEV)
    local_kv = prompt_kv[0]
    q_heads = tail_q[0].reshape(TAIL_DEV, KVH, GROUP, HD)
    start_peak = jnp.full((KVH, TAIL_DEV, GROUP), FLOOR, jnp.float32)
    piece = lax.all_gather(prompt_kv, "ctx", axis=1, tiled=True)
    peak = start_peak
    piece = piece[0]
    allowed = key_allowed(jnp.arange(piece.shape[0]), own_pos)

    def one_head(head):
        query = lax.dynamic_index_in_dim(q_heads, head, 1, keepdims=False)
        keys = lax.dynamic_slice_in_dim(piece, head * HD, HD, 1)
        values = lax.dynamic_slice_in_dim(piece, KVD + head * HD, HD, 1)
        scores = jnp.einsum("cgd,pd->cgp", query, keys, preferred_element_type=jnp.float32) * scale
        scores = jnp.where(allowed[:, None, :], scores, MASKED)
        old_peak = peak[head]
        new_peak = jnp.maximum(old_peak, jnp.max(scores, axis=-1))
        weights = jnp.exp(scores - new_peak[..., None])
        new_total = jnp.sum(weights, axis=-1)
        new_mixed = jnp.einsum("cgp,pd->cgd", weights, values, preferred_element_type=jnp.float32)
        return (new_peak, new_total, new_mixed)

    peak, total, mixed = lax.map(one_head, jnp.arange(KVH))
    prefill_out = (
        (mixed / total[..., None])
        .transpose(1, 0, 2, 3)
        .reshape(TAIL_DEV, QD)
        .astype(jnp.bfloat16)[None]
    )
    owners = dest_owner.reshape(NB)
    targets = dest_row.reshape(NB)
    slots = n_grp * per_owner
    same_owner = owners[:, None] == owners[None, :]
    earlier = jnp.arange(NB)[None, :] < jnp.arange(NB)[:, None]
    rank = jnp.sum(same_owner & earlier, axis=1)
    slot = owners * per_owner + rank
    match = slot[None, :] == jnp.arange(slots)[:, None]
    filled = jnp.any(match, axis=1)
    source = jnp.sum(jnp.where(match, jnp.arange(NB)[None, :], 0), axis=1)
    row_of = jnp.where(filled, jnp.sum(jnp.where(match, targets[None, :], 0), axis=1), -1)
    blocks = local_kv.reshape(NB, BLK, 2 * KVD)
    outgoing = jnp.where(filled[:, None, None], jnp.take(blocks, source, axis=0), 0)
    outgoing = outgoing.reshape(n_grp, per_owner * BLK, 2 * KVD)
    labels = row_of.astype(jnp.bfloat16).reshape(n_grp, per_owner)
    arrived, arrived_rows = (
        lax.all_to_all(outgoing, "grp", split_axis=0, concat_axis=0, tiled=True),
        lax.all_to_all(labels, "grp", split_axis=0, concat_axis=0, tiled=True),
    )
    q_rows = dec_q.reshape(ROW_GRP, 2, KVH, GROUP, HD)
    res_keys = res_kv[:, :, :KVD].reshape(ROW_GRP, RES_DEV, KVH, HD)
    res_values = res_kv[:, :, KVD:].reshape(ROW_GRP, RES_DEV, KVH, HD)
    live = ctx_pos * RES_DEV + jnp.arange(RES_DEV)[None, :] < lens[:, None]
    score_res = (
        jnp.einsum("rtkgd,rpkd->rtkgp", q_rows, res_keys, preferred_element_type=jnp.float32)
        * scale
    )
    score_res = jnp.where(live[:, None, None, None, :], score_res, MASKED)
    moved = arrived.reshape(slots, BLK, 2 * KVD)
    moved_rows = arrived_rows.reshape(slots).astype(jnp.int32)
    valid = moved_rows >= 0
    chosen = jnp.maximum(moved_rows, 0)
    q_slots = jnp.take(q_rows, chosen, axis=0)
    moved_keys = moved[:, :, :KVD].reshape(slots, BLK, KVH, HD)
    moved_values = moved[:, :, KVD:].reshape(slots, BLK, KVH, HD)
    score_moved = (
        jnp.einsum("stkgd,sbkd->stkgb", q_slots, moved_keys, preferred_element_type=jnp.float32)
        * scale
    )
    score_moved = jnp.where(valid[:, None, None, None, None], score_moved, MASKED)
    owner_match = moved_rows[None, :] == jnp.arange(ROW_GRP)[:, None]
    slot_peak = jnp.max(score_moved, axis=-1)
    moved_peak = jnp.max(
        jnp.where(owner_match[:, :, None, None, None], slot_peak[None], MASKED), axis=1
    )
    local_peak = jnp.maximum(jnp.maximum(jnp.max(score_res, axis=-1), moved_peak), FLOOR)
    weight_res = jnp.exp(score_res - local_peak[..., None])
    weight_moved = jnp.exp(score_moved - jnp.take(local_peak, chosen, axis=0)[..., None])
    one_hot = owner_match.astype(jnp.float32)
    part_total = jnp.sum(weight_res, axis=-1) + jnp.einsum(
        "rs,stkg->rtkg", one_hot, jnp.sum(weight_moved, axis=-1)
    )
    slot_mixed = jnp.einsum(
        "stkgb,sbkd->stkgd", weight_moved, moved_values, preferred_element_type=jnp.float32
    )
    part_mixed = jnp.einsum(
        "rtkgp,rpkd->rtkgd", weight_res, res_values, preferred_element_type=jnp.float32
    )
    part_mixed = part_mixed + jnp.einsum("rs,stkgd->rtkgd", one_hot, slot_mixed)
    part_peak = local_peak.reshape(ROW_GRP, 2, H)
    part_total = part_total.reshape(ROW_GRP, 2, H)
    part_mixed = part_mixed.reshape(ROW_GRP, 2, H, HD)
    heads_dev = H // n_ctx
    first_head = ctx_pos * heads_dev
    peak_all, total_all, mixed_all = merged((part_peak, part_total, part_mixed), "ctx", join_parts)
    top = lax.dynamic_slice_in_dim(peak_all, first_head, heads_dev, 2)
    row_total = lax.dynamic_slice_in_dim(total_all, first_head, heads_dev, 2)
    row_mixed = lax.dynamic_slice_in_dim(mixed_all, first_head, heads_dev, 2)
    own_heads = first_head + jnp.arange(heads_dev)
    key_head = own_heads // GROUP
    q_own = lax.dynamic_slice_in_dim(dec_q.reshape(ROW_GRP, 2, H, HD), first_head, heads_dev, 2)
    new_keys = jnp.take(new_kv[:, :, :KVD].reshape(ROW_GRP, 2, KVH, HD), key_head, axis=2)
    new_values = jnp.take(new_kv[:, :, KVD:].reshape(ROW_GRP, 2, KVH, HD), key_head, axis=2)
    score_new = (
        jnp.einsum("rthd,ruhd->rthu", q_own, new_keys, preferred_element_type=jnp.float32) * scale
    )
    causal = jnp.arange(2)[None, :] <= jnp.arange(2)[:, None]
    score_new = jnp.where(causal[None, :, None, :], score_new, MASKED)
    final_peak = jnp.maximum(top, jnp.max(score_new, axis=-1))
    fade_old = jnp.exp(top - final_peak)
    weight_new = jnp.exp(score_new - final_peak[..., None])
    final_total = row_total * fade_old + jnp.sum(weight_new, axis=-1)
    final_mixed = row_mixed * fade_old[..., None] + jnp.einsum(
        "rthu,ruhd->rthd", weight_new, new_values, preferred_element_type=jnp.float32
    )
    decode_out = (
        (final_mixed / final_total[..., None])
        .astype(jnp.bfloat16)
        .reshape(ROW_GRP, 2, heads_dev * HD)
    )
    return (prefill_out, decode_out)


def solution(mesh):
    return jax.shard_map(
        local,
        mesh=mesh,
        in_specs=(
            P("grp", "ctx", None),
            P("grp", "ctx", None),
            P("grp", "ctx", None, None),
            P("grp", "ctx", None),
            P("grp", None, None),
            P("grp", None, None),
            P("grp", "ctx", None),
            P("grp"),
        ),
        out_specs=(P("grp", "ctx", None), P("grp", None, "ctx")),
        check_vma=False,
    )
```

profile of v0, /device:TPU:1, one launch (start us, length us, event | category | flops | bytes accessed | tf_op | source)
XLA Modules:
  0.0 536.1 jit_solution(9862161308717518359)
XLA Ops:
  7.2 0.9 convert_reduce_fusion
  8.8 0.7 select_reduce_fusion.2
  9.6 0.7 convert_element_type.76
  10.3 7.3 %all-to-all-start = ((bf16[16,1,5]{2,1,0:T(2,128)(2,1)}), bf16[16,1,5]{2,1,0:T(2,128)(2,1)S(1)}, u32[]{:S(2)}, u32[]{:S(2)}) async-start(bf16[16,1,5]{2,1,0:T(2,128)(2,1)} %convert_element_type.76), calls=%async_computation | async-start | bytes 16384 | tf_op jit(solution)/shard_map/all_to_all | solution.py:101
  18.2 7.3 %gather_fusion = bf16[80,16,2048]{2,1,0:T(8,128)(2,1)} fusion(bf16[35,16,2048]{2,1,0:T(8,128)(2,1)} %bitcast.169, s32[1024]{0:T(1024)S(1)} %pad_clamp_fusion.2), kind=kCustom, calls=%fused_computation.2 | custom fusion | bytes 10486080 | tf_op jit(solution)/shard_map/jit(_take)/gather | solution.py:96
  25.5 5.5 %fusion.20 = bf16[16,80,2048]{2,1,0:T(8,128)(2,1)} fusion(pred[16,80]{1,0:T(8,128)(4,1)S(1)} %broadcast_in_dim.227, pred[16,80]{1,0:T(8,128)(4,1)S(1)} %broadcast_in_dim.223, bf16[16,80,2048]{2,1,0:T(8,128)(2,1)} %bitcast.170), kind=kLoop, calls=%fused_computation.39 | loop fusion | flops 5242880 | bytes 10488320 | tf_op jit(solution)/shard_map/jit(_where)/select_n | solution.py:96
  31.1 5.9 %all-to-all-start.1 = ((bf16[16,80,2048]{2,1,0:T(8,128)(2,1)}), bf16[16,80,2048]{2,1,0:T(8,128)(2,1)}, u32[]{:S(2)}, u32[]{:S(2)}) async-start(bf16[16,80,2048]{2,1,0:T(8,128)(2,1)} %fusion.20), calls=%async_computation.1 | async-start | bytes 10485760 | tf_op jit(solution)/shard_map/all_to_all | solution.py:100
  37.3 1.8 fusion.84
  39.8 1.3 copy.276
  41.2 1.1 fusion.86
  42.6 2.6 gather_fusion.1
  45.1 64.0 %all-to-all-done.1 = bf16[16,80,2048]{2,1,0:T(8,128)(2,1)} async-done(((bf16[16,80,2048]{2,1,0:T(8,128)(2,1)}), bf16[16,80,2048]{2,1,0:T(8,128)(2,1)}, u32[]{:S(2)}, u32[]{:S(2)}) %all-to-all-start.1) | async-done | bytes 5242912 | tf_op jit(solution)/shard_map/all_to_all | solution.py:100
  109.2 3.1 fusion.83
  113.1 1.5 copy-done.3
  114.7 3.9 bitcast_reduce_fusion
  121.4 1.0 slice-done
  122.7 2.5 fusion.34
  125.2 1.5 fusion.21
  127.4 0.7 copy.325
  128.2 0.7 all-gather.3.cloned.1.call-update
  131.3 0.9 fusion.87
  132.3 28.1 %all_gather.13 = f32[8,4,2,64]{3,1,2,0:T(4,128)S(1)} all-gather(f32[1,4,2,64]{3,1,2,0:T(4,128)S(1)} %copy.232), channel_id=1, replica_groups=mesh['ctx'=8,'grp'=16] {'ctx'}, dimensions={0}, use_global_device_ids=true | all-gather | bytes 18432 | tf_op jit(solution)/shard_map/all_gather | solution.py:25
  160.8 5.6 %fusion.25 = bf16[80,2,8,8]{3,1,2,0:T(2,128)(2,1)S(1)} fusion(f32[80,8,16,2,8]{2,4,3,1,0:T(8,128)} %get-tuple-element.311, f32[80,2,8,8]{3,1,2,0:T(2,128)S(1)} %copy-done.2, pred[80]{0:T(512)(128)(4,1)S(1)} %copy-done.11), kind=kLoop, calls=%fused_computation.44 | loop fusion | flops 645120 | bytes 716880 | tf_op jit(solution)/shard_map/reduce_sum | solution.py:134
  166.7 28.0 %all_gather.14 = f32[8,4,2,64]{3,1,2,0:T(4,128)S(1)} all-gather(f32[1,4,2,64]{3,1,2,0:T(4,128)S(1)} %copy.238), channel_id=1, replica_groups=mesh['ctx'=8,'grp'=16] {'ctx'}, dimensions={0}, use_global_device_ids=true | all-gather | bytes 18432 | tf_op jit(solution)/shard_map/all_gather | solution.py:25
  194.8 1.6 slice.65
  196.4 1.0 slice_bitcast_fusion
  197.4 2.3 while.29
  200.2 1.6 fusion.47
  201.8 190.6 %all-gather.3.cloned.1.call-done = bf16[1,4480,2048]{2,1,0:T(8,128)(2,1)} async-done(((bf16[1,560,2048]{2,1,0:T(8,128)(2,1)}), bf16[1,4480,2048]{2,1,0:T(8,128)(2,1)}) %all-gather.3.cloned.1.call-update) | async-done | bytes 18350096 | tf_op jit(solution)/shard_map/all_gather | solution.py:59
  392.4 133.4 %while.30 = (s32[]{:T(128)}, f32[8,64,8]{2,1,0:T(8,128)S(1)}, f32[8,64,8,128]{3,2,1,0:T(8,128)}, s32[8]{0:T(128)S(1)}, bf16[64,8,8,128]{3,2,1,0:T(8,128)(2,1)S(1...) while((s32[]{:T(128)}, f32[8,64,8]{2,1,0:T(8,128)S(1)}, ...), condition=%wide.region_3.4_spmd.clone, body=%wide.region_0.3_spmd.clone.sunk | while | flops 1188453888 | bytes 67582032 | solution.py:77
  395.8 3.6 fusion.99
  399.4 1.4 fusion.100
  400.8 2.2 copy-done
  403.0 6.0 %fusion.101 = f32[8,64,8,128]{3,2,1,0:T(8,128)} fusion(f32[8,64,8,128]{3,2,1,0:T(8,128)} %get-tuple-element.441, s32[]{:T(128)S(6)} %copy.333, f32[64,8,4480]{2,1,0:T(8,128)} %copy-done, f32[64,8]{1,0:T(8,128)S(1)} %broadcast_maximum_fusion.2, bf16[4480,2048]{1,0:T(8,128)(2,1)} %get-tuple-element.459, s32[]{:T(128)S(6)} %select_n.253), kind=kOutput, calls=%fused_computation.23.clone.1 | convolution fusion | flops 589496320 | bytes 10586120 | tf_op jit(solution)/shard_map/while/body/eval_jaxpr/cgp,pd->cgd/dot_general | solution.py:74
  412.4 3.6 fusion.99
  416.0 1.4 fusion.100
  417.4 2.2 copy-done
  419.6 6.1 %fusion.101 = f32[8,64,8,128]{3,2,1,0:T(8,128)} fusion(f32[8,64,8,128]{3,2,1,0:T(8,128)} %get-tuple-element.441, s32[]{:T(128)S(6)} %copy.333, f32[64,8,4480]{2,1,0:T(8,128)} %copy-done, f32[64,8]{1,0:T(8,128)S(1)} %broadcast_maximum_fusion.2, bf16[4480,2048]{1,0:T(8,128)(2,1)} %get-tuple-element.459, s32[]{:T(128)S(6)} %select_n.253), kind=kOutput, calls=%fused_computation.23.clone.1 | convolution fusion | flops 589496320 | bytes 10586120 | tf_op jit(solution)/shard_map/while/body/eval_jaxpr/cgp,pd->cgd/dot_general | solution.py:74
  429.1 3.6 fusion.99
  432.7 1.4 fusion.100
  434.1 2.2 copy-done
  436.3 6.2 %fusion.101 = f32[8,64,8,128]{3,2,1,0:T(8,128)} fusion(f32[8,64,8,128]{3,2,1,0:T(8,128)} %get-tuple-element.441, s32[]{:T(128)S(6)} %copy.333, f32[64,8,4480]{2,1,0:T(8,128)} %copy-done, f32[64,8]{1,0:T(8,128)S(1)} %broadcast_maximum_fusion.2, bf16[4480,2048]{1,0:T(8,128)(2,1)} %get-tuple-element.459, s32[]{:T(128)S(6)} %select_n.253), kind=kOutput, calls=%fused_computation.23.clone.1 | convolution fusion | flops 589496320 | bytes 10586120 | tf_op jit(solution)/shard_map/while/body/eval_jaxpr/cgp,pd->cgd/dot_general | solution.py:74
  445.9 3.6 fusion.99
  449.5 1.4 fusion.100
  450.9 2.2 copy-done
  453.1 6.1 %fusion.101 = f32[8,64,8,128]{3,2,1,0:T(8,128)} fusion(f32[8,64,8,128]{3,2,1,0:T(8,128)} %get-tuple-element.441, s32[]{:T(128)S(6)} %copy.333, f32[64,8,4480]{2,1,0:T(8,128)} %copy-done, f32[64,8]{1,0:T(8,128)S(1)} %broadcast_maximum_fusion.2, bf16[4480,2048]{1,0:T(8,128)(2,1)} %get-tuple-element.459, s32[]{:T(128)S(6)} %select_n.253), kind=kOutput, calls=%fused_computation.23.clone.1 | convolution fusion | flops 589496320 | bytes 10586120 | tf_op jit(solution)/shard_map/while/body/eval_jaxpr/cgp,pd->cgd/dot_general | solution.py:74
  462.6 3.6 fusion.99
  466.2 1.4 fusion.100
  467.6 2.2 copy-done
  469.8 6.0 %fusion.101 = f32[8,64,8,128]{3,2,1,0:T(8,128)} fusion(f32[8,64,8,128]{3,2,1,0:T(8,128)} %get-tuple-element.441, s32[]{:T(128)S(6)} %copy.333, f32[64,8,4480]{2,1,0:T(8,128)} %copy-done, f32[64,8]{1,0:T(8,128)S(1)} %broadcast_maximum_fusion.2, bf16[4480,2048]{1,0:T(8,128)(2,1)} %get-tuple-element.459, s32[]{:T(128)S(6)} %select_n.253), kind=kOutput, calls=%fused_computation.23.clone.1 | convolution fusion | flops 589496320 | bytes 10586120 | tf_op jit(solution)/shard_map/while/body/eval_jaxpr/cgp,pd->cgd/dot_general | solution.py:74
  479.2 3.6 fusion.99
  482.8 1.4 fusion.100
  484.2 2.2 copy-done
  486.4 6.1 %fusion.101 = f32[8,64,8,128]{3,2,1,0:T(8,128)} fusion(f32[8,64,8,128]{3,2,1,0:T(8,128)} %get-tuple-element.441, s32[]{:T(128)S(6)} %copy.333, f32[64,8,4480]{2,1,0:T(8,128)} %copy-done, f32[64,8]{1,0:T(8,128)S(1)} %broadcast_maximum_fusion.2, bf16[4480,2048]{1,0:T(8,128)(2,1)} %get-tuple-element.459, s32[]{:T(128)S(6)} %select_n.253), kind=kOutput, calls=%fused_computation.23.clone.1 | convolution fusion | flops 589496320 | bytes 10586120 | tf_op jit(solution)/shard_map/while/body/eval_jaxpr/cgp,pd->cgd/dot_general | solution.py:74
  495.9 3.6 fusion.99
  499.5 1.4 fusion.100
  500.9 2.2 copy-done
  503.1 6.1 %fusion.101 = f32[8,64,8,128]{3,2,1,0:T(8,128)} fusion(f32[8,64,8,128]{3,2,1,0:T(8,128)} %get-tuple-element.441, s32[]{:T(128)S(6)} %copy.333, f32[64,8,4480]{2,1,0:T(8,128)} %copy-done, f32[64,8]{1,0:T(8,128)S(1)} %broadcast_maximum_fusion.2, bf16[4480,2048]{1,0:T(8,128)(2,1)} %get-tuple-element.459, s32[]{:T(128)S(6)} %select_n.253), kind=kOutput, calls=%fused_computation.23.clone.1 | convolution fusion | flops 589496320 | bytes 10586120 | tf_op jit(solution)/shard_map/while/body/eval_jaxpr/cgp,pd->cgd/dot_general | solution.py:74
  512.5 3.6 fusion.99
  516.2 1.4 fusion.100
  517.6 2.2 copy-done
  519.7 6.0 %fusion.101 = f32[8,64,8,128]{3,2,1,0:T(8,128)} fusion(f32[8,64,8,128]{3,2,1,0:T(8,128)} %get-tuple-element.441, s32[]{:T(128)S(6)} %copy.333, f32[64,8,4480]{2,1,0:T(8,128)} %copy-done, f32[64,8]{1,0:T(8,128)S(1)} %broadcast_maximum_fusion.2, bf16[4480,2048]{1,0:T(8,128)(2,1)} %get-tuple-element.459, s32[]{:T(128)S(6)} %select_n.253), kind=kOutput, calls=%fused_computation.23.clone.1 | convolution fusion | flops 589496320 | bytes 10586120 | tf_op jit(solution)/shard_map/while/body/eval_jaxpr/cgp,pd->cgd/dot_general | solution.py:74
  525.8 2.0 fusion.48
  528.0 1.3 convert_element_type.67
  (166 shorter events, 19.7 us)
Async XLA Ops:
  10.3 20.8 %all-to-all-start = ((bf16[16,1,5]{2,1,0:T(2,128)(2,1)}), bf16[16,1,5]{2,1,0:T(2,128)(2,1)S(1)}, u32[]{:S(2)}, u32[]{:S(2)}) async-start(bf16[16,1,5]{2,1,0:T(2,128)(2,1)} %convert_element_type.76), calls=%async_computation | async-start | bytes 16384 | tf_op jit(solution)/shard_map/all_to_all | solution.py:101
  31.0 6.1 %copy-start.8 = (bf16[4,2,8192]{2,1,0:T(2,128)(2,1)S(1)}, bf16[4,2,8192]{2,1,0:T(2,128)(2,1)}, u32[]{:S(2)}) copy-start(bf16[4,2,8192]{2,1,0:T(2,128)(2,1)} %param.18) | copy-start | bytes 393220
  31.1 78.1 %all-to-all-start.1 = ((bf16[16,80,2048]{2,1,0:T(8,128)(2,1)}), bf16[16,80,2048]{2,1,0:T(8,128)(2,1)}, u32[]{:S(2)}, u32[]{:S(2)}) async-start(bf16[16,80,2048]{2,1,0:T(8,128)(2,1)} %fusion.20), calls=%async_computation.1 | async-start | bytes 10485760 | tf_op jit(solution)/shard_map/all_to_all | solution.py:100
  36.9 157.8 %all-gather.5.cloned.1.call-start = ((), (), s32[]{:S(2)}) async-start(), calls=%async_computation.3 | async-start | bytes 2359296 | tf_op jit(solution)/shard_map/all_gather | solution.py:25
  39.1 2.0 copy-start.12
  45.1 76.1 %copy-start.10 = (pred[80]{0:T(512)(128)(4,1)}, pred[80]{0:T(512)(128)(4,1)S(1)}, u32[]{:S(2)}) copy-start(pred[80]{0:T(512)(128)(4,1)S(1)} %get-tuple-element.308) | copy-start | bytes 244
  112.9 1.7 copy-start.3
  119.9 2.4 slice-start
  120.3 1.1 copy-start.1
  120.3 2.4 slice-start.1
  125.2 1.5 copy-start.5
  125.2 1.5 copy-start.6
  126.7 2.3 copy-start.4
  127.4 1.8 copy-start.9
  128.2 32.6 %copy-start.2 = (f32[80,2,8,8]{3,1,2,0:T(2,128)S(1)}, f32[80,2,8,8]{3,1,2,0:T(2,128)}, u32[]{:S(2)}) copy-start(f32[80,2,8,8]{3,1,2,0:T(2,128)} %copy-done.1) | copy-start | bytes 122884
  128.2 32.6 %copy-start.11 = (pred[80]{0:T(512)(128)(4,1)S(1)}, pred[80]{0:T(512)(128)(4,1)}, u32[]{:S(2)}) copy-start(pred[80]{0:T(512)(128)(4,1)} %copy-done.10) | copy-start | bytes 244
  128.2 264.2 %all-gather.3.cloned.1.call-start = ((), (), s32[]{:S(2)}) async-start(), calls=%async_computation.2 | async-start | bytes 20643840 | tf_op jit(solution)/shard_map/all_gather | solution.py:59
  160.5 6.0 %copy-start.7 = (f32[8,4,2,64]{3,1,2,0:T(4,128)}, f32[8,4,2,64]{3,1,2,0:T(4,128)S(1)}, u32[]{:S(2)}) copy-start(f32[8,4,2,64]{3,1,2,0:T(4,128)S(1)} %all_gather.13) | copy-start | bytes 49156
  166.6 30.7 %slice-start.2 = ((f32[8,4,2,64]{3,1,2,0:T(4,128)}), f32[7,4,2,64]{3,1,2,0:T(4,128)S(1)}, s32[]{:S(2)}) async-start(f32[8,4,2,64]{3,1,2,0:T(4,128)} %copy-done.7), calls=%async_computation.6 | async-start | bytes 57344 | tf_op jit(solution)/shard_map/slice | solution.py:27
  399.4 3.6 copy-start
  416.0 3.6 copy-start
  432.7 3.6 copy-start
  449.5 3.6 copy-start
  466.2 3.6 copy-start
  482.8 3.6 copy-start
  499.5 3.6 copy-start
  516.2 3.6 copy-start
Sparse Core Ops, SparseCore 0:
  128.3 61.8 all-gather.4
  192.5 199.7 all-gather.2
where the time goes:
time: 537 us; the launch traced here: 536 us
  waiting for transfers between devices  255 us (47%)
  matrix products  89.7 us (17%)
  blocking collectives  56.1 us (10%)
  local copies, waits for them, and re-layouts  53.6 us (10%)
  other arithmetic  32.1 us (6%)
  loops' own time  21.2 us (4%)
  between operations  14.6 us (3%)
  starting transfers between devices  13.5 us (3%)
    all_gather x1, waiting for transfers between devices, local(): piece = lax.all_gather(prompt_kv, 'ctx', axis=1, tiled=True)  191 us
    all_to_all x1, waiting for transfers between devices, local(): lax.all_to_all(outgoing, 'grp', split_axis=0, concat_axis=0, tiled=True)  64 us
    all_gather x2, blocking collectives, merged(): pieces = jax.tree.map(lambda part: lax.all_gather(part, axis), value)  56.1 us
    dot_general x8, matrix products, one_head(): jnp.einsum('cgp,pd->cgd', weights, values, preferred_element_type=jnp.flo...  48.5 us
    dot_general x8, matrix products, one_head(): jnp.einsum('cgd,pd->cgp', query, keys, preferred_element_type=jnp.float32)  28.9 us
    another operation x1, loops' own time, local(): peak, total, mixed = lax.map(one_head, jnp.arange(KVH))  21 us
    while x16, local copies, waits for them, and re-layouts  17.3 us
    reduce_sum x8, other arithmetic, one_head(): new_total = jnp.sum(weights, axis=-1)  11.2 us
  transfers between devices with their start and end apart: 4, of which 2 were waited for; matrix products, arithmetic and copies ran while one was open for 7% of the time, Pallas kernels for 0%

commit v1 on v0

--- a/solution.py
+++ b/solution.py
@@ -56,7 +56,9 @@
     local_kv = prompt_kv[0]
     q_heads = tail_q[0].reshape(TAIL_DEV, KVH, GROUP, HD)
     start_peak = jnp.full((KVH, TAIL_DEV, GROUP), FLOOR, jnp.float32)
-    piece = lax.all_gather(prompt_kv, "ctx", axis=1, tiled=True)
+    piece = jnp.concatenate(
+        lax.all_to_all(jnp.stack([prompt_kv] * lax.axis_size("ctx")), "ctx", 0, 0), axis=1
+    )
     peak = start_peak
     piece = piece[0]
     allowed = key_allowed(jnp.arange(piece.shape[0]), own_pos)

time: 537 us -> 584 us (1.088)
  the two profiles are of different devices: /device:TPU:1 before, /device:TPU:0 now
where the time goes in v1:
time: 584 us; the launch traced here: 582 us
  blocking collectives  344 us (59%)
  matrix products  109 us (19%)
  local copies, waits for them, and re-layouts  47 us (8%)
  other arithmetic  32.7 us (6%)
  loops' own time  21.1 us (4%)
  between operations  14.7 us (3%)
  starting transfers between devices  13.7 us (2%)
    all_gather x2, blocking collectives, merged(): pieces = jax.tree.map(lambda part: lax.all_gather(part, axis), value)  277 us
    all_to_all x1, blocking collectives, local(): lax.all_to_all(outgoing, 'grp', split_axis=0, concat_axis=0, tiled=True)  67.4 us
    dot_general x8, matrix products, one_head(): jnp.einsum('cgp,pd->cgd', weights, values, preferred_element_type=jnp.flo...  49.1 us
    dot_general x8, matrix products, one_head(): jnp.einsum('cgd,pd->cgp', query, keys, preferred_element_type=jnp.float32)  48.2 us
    another operation x1, loops' own time, local(): peak, total, mixed = lax.map(one_head, jnp.arange(KVH))  20.9 us
  transfers between devices with their start and end apart: 3, of which 0 were waited for; matrix products, arithmetic and copies ran while one was open for 9% of the time, Pallas kernels for 0%

profile of v1, /device:TPU:0, one launch (start us, length us, event | category | flops | bytes accessed | tf_op | source)
XLA Modules:
  0.0 582.5 jit_solution(15634565578093858982)
XLA Ops:
  7.2 0.9 convert_reduce_fusion
  8.1 0.7 multiply_add_fusion.1
  8.8 0.7 select_reduce_fusion.2
  9.6 0.7 convert_element_type.76
  10.3 6.0 %all-to-all-start.1 = ((bf16[16,1,5]{2,1,0:T(2,128)(2,1)}), bf16[16,1,5]{2,1,0:T(2,128)(2,1)S(1)}, u32[]{:S(2)}, u32[]{:S(2)}) async-start(bf16[16,1,5]{2,1,0:T(2,128)(2,1)} %convert_element_type.76), calls=%async_computation.1 | async-start | bytes 16384 | tf_op jit(solution)/shard_map/all_to_all | solution.py:103
  16.9 7.3 %gather_fusion = bf16[80,16,2048]{2,1,0:T(8,128)(2,1)} fusion(bf16[35,16,2048]{2,1,0:T(8,128)(2,1)} %bitcast.170, s32[1024]{0:T(1024)S(1)} %pad_clamp_fusion.2), kind=kCustom, calls=%fused_computation.2 | custom fusion | bytes 10486080 | tf_op jit(solution)/shard_map/jit(_take)/gather | solution.py:98
  24.2 5.5 fusion.20
  29.8 67.4 %all_to_all.16 = bf16[16,80,2048]{2,1,0:T(8,128)(2,1)} all-to-all(bf16[16,80,2048]{2,1,0:T(8,128)(2,1)} %fusion.20), channel_id=1, replica_groups=mesh['ctx'=8,'grp'=16] {'grp'}, dimensions={0} | all-to-all | bytes 10485760 | tf_op jit(solution)/shard_map/all_to_all | solution.py:102
  97.1 6.5 %stack.2 = bf16[8,1,560,2048]{3,2,1,0:T(8,128)(2,1)} broadcast(bf16[560,2048]{1,0:T(8,128)(2,1)S(1)} %bitcast.171), dimensions={2,3} | broadcast | bytes 20643840 | tf_op jit(solution)/shard_map/stack | solution.py:60
  103.6 7.4 %all-to-all-start = ((bf16[8,1,560,2048]{3,2,1,0:T(8,128)(2,1)}), bf16[8,1,560,2048]{3,2,1,0:T(8,128)(2,1)}, u32[]{:S(2)}, u32[]{:S(2)}) async-start(bf16[8,1,560,2048]{3,2,1,0:T(8,128)(2,1)} %stack.2), calls=%async_computation | async-start | bytes 36700160 | tf_op jit(solution)/shard_map/all_to_all | solution.py:60
  111.5 1.8 fusion.84
  113.3 0.7 copy.275
  114.0 1.3 copy.276
  115.4 1.1 fusion.86
  116.7 2.6 gather_fusion.1
  119.3 3.1 fusion.83
  122.4 0.6 copy.278
  123.3 1.5 copy-done.4
  124.8 3.8 bitcast_reduce_fusion
  129.2 0.7 gather_fusion.2
  130.4 0.7 copy.279
  131.5 1.0 slice-done
  132.8 2.5 fusion.34
  135.3 1.5 fusion.21
  136.8 0.7 fusion.39
  137.5 0.7 copy.325
  139.9 0.6 iota_add_fusion.1
  140.5 0.7 select_bitcast_fusion
  141.2 0.8 fusion.87
  142.4 5.6 fusion.25
  148.4 242.1 %all_gather.10 = f32[8,4,2,64]{3,1,2,0:T(4,128)S(1)} all-gather(f32[1,4,2,64]{3,1,2,0:T(4,128)S(1)} %copy.238), channel_id=1, replica_groups=mesh['ctx'=8,'grp'=16] {'ctx'}, dimensions={0}, use_global_device_ids=true | all-gather | bytes 18432 | tf_op jit(solution)/shard_map/all_gather | solution.py:25
  390.5 34.5 %all_gather.9 = f32[8,4,2,64]{3,1,2,0:T(4,128)S(1)} all-gather(f32[1,4,2,64]{3,1,2,0:T(4,128)S(1)} %copy.232), channel_id=1, replica_groups=mesh['ctx'=8,'grp'=16] {'ctx'}, dimensions={0}, use_global_device_ids=true | all-gather | bytes 18432 | tf_op jit(solution)/shard_map/all_gather | solution.py:25
  425.1 1.6 slice.65
  426.7 1.0 slice_bitcast_fusion
  427.7 2.3 while.29
  430.6 1.6 fusion.47
  432.1 139.9 %while.30 = (s32[]{:T(128)}, f32[8,64,8]{2,1,0:T(8,128)S(1)}, f32[8,64,8,128]{3,2,1,0:T(8,128)}, s32[8]{0:T(128)S(1)}, bf16[64,8,8,128]{3,2,1,0:T(8,128)(2,1)S(1...) while((s32[]{:T(128)}, f32[8,64,8]{2,1,0:T(8,128)S(1)}, ...), condition=%wide.region_3.4_spmd.clone, body=%wide.region_0.3_spmd.clone.sunk | while | flops 1188453888 | bytes 67582528 | solution.py:79
  435.6 6.0 %fusion.99 = (f32[64,8]{1,0:T(8,128)S(1)}, f32[64,8,4480]{2,1,0:T(8,128)}) fusion(bf16[4480,2048]{1,0:T(8,128)(2,1)} %get-tuple-element.459, s32[]{:T(128)S(6)} %select_n.251, bf16[64,8,8,128]{3,2,1,0:T(8,128)(2,1)S(1)} %get-tuple-element.458, s32[]{:T(128)S(6)} %select_n.252, pred[64,4480]{1,0:T(8,128)(4,1)S(1)} %broadcast_compare_fusion.4), kind=kOutput, calls=%fused_computation.151.clone.1 | convolution fusion | flops 594083328 | bytes 10741768 | tf_op jit(solution)/shard_map/while/body/eval_jaxpr/cgd,pd->cgp/dot_general | solution.py:70
  441.6 6.1 %fusion.101 = f32[8,64,8,128]{3,2,1,0:T(8,128)} fusion(f32[8,64,8,128]{3,2,1,0:T(8,128)} %get-tuple-element.441, s32[]{:T(128)} %get-tuple-element.439, f32[64,8,4480]{2,1,0:T(8,128)} %get-tuple-element.422, f32[64,8]{1,0:T(8,128)S(1)} %broadcast_maximum_fusion.2, bf16[4480,2048]{1,0:T(8,128)(2,1)} %get-tuple-element.459, s32[]{:T(128)S(6)} %select_n.253), kind=kOutput, calls=%fused_computation.23.clone.1 | convolution fusion | flops 589496320 | bytes 10586628 | tf_op jit(solution)/shard_map/while/body/eval_jaxpr/cgp,pd->cgd/dot_general | solution.py:76
  448.2 1.4 fusion.100
  449.6 0.6 dynamic_slice.96
  453.1 6.0 %fusion.99 = (f32[64,8]{1,0:T(8,128)S(1)}, f32[64,8,4480]{2,1,0:T(8,128)}) fusion(bf16[4480,2048]{1,0:T(8,128)(2,1)} %get-tuple-element.459, s32[]{:T(128)S(6)} %select_n.251, bf16[64,8,8,128]{3,2,1,0:T(8,128)(2,1)S(1)} %get-tuple-element.458, s32[]{:T(128)S(6)} %select_n.252, pred[64,4480]{1,0:T(8,128)(4,1)S(1)} %broadcast_compare_fusion.4), kind=kOutput, calls=%fused_computation.151.clone.1 | convolution fusion | flops 594083328 | bytes 10741768 | tf_op jit(solution)/shard_map/while/body/eval_jaxpr/cgd,pd->cgp/dot_general | solution.py:70
  459.1 6.2 %fusion.101 = f32[8,64,8,128]{3,2,1,0:T(8,128)} fusion(f32[8,64,8,128]{3,2,1,0:T(8,128)} %get-tuple-element.441, s32[]{:T(128)} %get-tuple-element.439, f32[64,8,4480]{2,1,0:T(8,128)} %get-tuple-element.422, f32[64,8]{1,0:T(8,128)S(1)} %broadcast_maximum_fusion.2, bf16[4480,2048]{1,0:T(8,128)(2,1)} %get-tuple-element.459, s32[]{:T(128)S(6)} %select_n.253), kind=kOutput, calls=%fused_computation.23.clone.1 | convolution fusion | flops 589496320 | bytes 10586628 | tf_op jit(solution)/shard_map/while/body/eval_jaxpr/cgp,pd->cgd/dot_general | solution.py:76
  465.7 1.4 fusion.100
  470.5 6.0 %fusion.99 = (f32[64,8]{1,0:T(8,128)S(1)}, f32[64,8,4480]{2,1,0:T(8,128)}) fusion(bf16[4480,2048]{1,0:T(8,128)(2,1)} %get-tuple-element.459, s32[]{:T(128)S(6)} %select_n.251, bf16[64,8,8,128]{3,2,1,0:T(8,128)(2,1)S(1)} %get-tuple-element.458, s32[]{:T(128)S(6)} %select_n.252, pred[64,4480]{1,0:T(8,128)(4,1)S(1)} %broadcast_compare_fusion.4), kind=kOutput, calls=%fused_computation.151.clone.1 | convolution fusion | flops 594083328 | bytes 10741768 | tf_op jit(solution)/shard_map/while/body/eval_jaxpr/cgd,pd->cgp/dot_general | solution.py:70
  476.6 6.2 %fusion.101 = f32[8,64,8,128]{3,2,1,0:T(8,128)} fusion(f32[8,64,8,128]{3,2,1,0:T(8,128)} %get-tuple-element.441, s32[]{:T(128)} %get-tuple-element.439, f32[64,8,4480]{2,1,0:T(8,128)} %get-tuple-element.422, f32[64,8]{1,0:T(8,128)S(1)} %broadcast_maximum_fusion.2, bf16[4480,2048]{1,0:T(8,128)(2,1)} %get-tuple-element.459, s32[]{:T(128)S(6)} %select_n.253), kind=kOutput, calls=%fused_computation.23.clone.1 | convolution fusion | flops 589496320 | bytes 10586628 | tf_op jit(solution)/shard_map/while/body/eval_jaxpr/cgp,pd->cgd/dot_general | solution.py:76
  483.2 1.4 fusion.100
  488.0 6.0 %fusion.99 = (f32[64,8]{1,0:T(8,128)S(1)}, f32[64,8,4480]{2,1,0:T(8,128)}) fusion(bf16[4480,2048]{1,0:T(8,128)(2,1)} %get-tuple-element.459, s32[]{:T(128)S(6)} %select_n.251, bf16[64,8,8,128]{3,2,1,0:T(8,128)(2,1)S(1)} %get-tuple-element.458, s32[]{:T(128)S(6)} %select_n.252, pred[64,4480]{1,0:T(8,128)(4,1)S(1)} %broadcast_compare_fusion.4), kind=kOutput, calls=%fused_computation.151.clone.1 | convolution fusion | flops 594083328 | bytes 10741768 | tf_op jit(solution)/shard_map/while/body/eval_jaxpr/cgd,pd->cgp/dot_general | solution.py:70
  494.1 6.1 %fusion.101 = f32[8,64,8,128]{3,2,1,0:T(8,128)} fusion(f32[8,64,8,128]{3,2,1,0:T(8,128)} %get-tuple-element.441, s32[]{:T(128)} %get-tuple-element.439, f32[64,8,4480]{2,1,0:T(8,128)} %get-tuple-element.422, f32[64,8]{1,0:T(8,128)S(1)} %broadcast_maximum_fusion.2, bf16[4480,2048]{1,0:T(8,128)(2,1)} %get-tuple-element.459, s32[]{:T(128)S(6)} %select_n.253), kind=kOutput, calls=%fused_computation.23.clone.1 | convolution fusion | flops 589496320 | bytes 10586628 | tf_op jit(solution)/shard_map/while/body/eval_jaxpr/cgp,pd->cgd/dot_general | solution.py:76
  500.7 1.4 fusion.100
  505.5 6.0 %fusion.99 = (f32[64,8]{1,0:T(8,128)S(1)}, f32[64,8,4480]{2,1,0:T(8,128)}) fusion(bf16[4480,2048]{1,0:T(8,128)(2,1)} %get-tuple-element.459, s32[]{:T(128)S(6)} %select_n.251, bf16[64,8,8,128]{3,2,1,0:T(8,128)(2,1)S(1)} %get-tuple-element.458, s32[]{:T(128)S(6)} %select_n.252, pred[64,4480]{1,0:T(8,128)(4,1)S(1)} %broadcast_compare_fusion.4), kind=kOutput, calls=%fused_computation.151.clone.1 | convolution fusion | flops 594083328 | bytes 10741768 | tf_op jit(solution)/shard_map/while/body/eval_jaxpr/cgd,pd->cgp/dot_general | solution.py:70
  511.6 6.1 %fusion.101 = f32[8,64,8,128]{3,2,1,0:T(8,128)} fusion(f32[8,64,8,128]{3,2,1,0:T(8,128)} %get-tuple-element.441, s32[]{:T(128)} %get-tuple-element.439, f32[64,8,4480]{2,1,0:T(8,128)} %get-tuple-element.422, f32[64,8]{1,0:T(8,128)S(1)} %broadcast_maximum_fusion.2, bf16[4480,2048]{1,0:T(8,128)(2,1)} %get-tuple-element.459, s32[]{:T(128)S(6)} %select_n.253), kind=kOutput, calls=%fused_computation.23.clone.1 | convolution fusion | flops 589496320 | bytes 10586628 | tf_op jit(solution)/shard_map/while/body/eval_jaxpr/cgp,pd->cgd/dot_general | solution.py:76
  518.2 1.4 fusion.100
  523.0 6.0 %fusion.99 = (f32[64,8]{1,0:T(8,128)S(1)}, f32[64,8,4480]{2,1,0:T(8,128)}) fusion(bf16[4480,2048]{1,0:T(8,128)(2,1)} %get-tuple-element.459, s32[]{:T(128)S(6)} %select_n.251, bf16[64,8,8,128]{3,2,1,0:T(8,128)(2,1)S(1)} %get-tuple-element.458, s32[]{:T(128)S(6)} %select_n.252, pred[64,4480]{1,0:T(8,128)(4,1)S(1)} %broadcast_compare_fusion.4), kind=kOutput, calls=%fused_computation.151.clone.1 | convolution fusion | flops 594083328 | bytes 10741768 | tf_op jit(solution)/shard_map/while/body/eval_jaxpr/cgd,pd->cgp/dot_general | solution.py:70
  529.0 6.1 %fusion.101 = f32[8,64,8,128]{3,2,1,0:T(8,128)} fusion(f32[8,64,8,128]{3,2,1,0:T(8,128)} %get-tuple-element.441, s32[]{:T(128)} %get-tuple-element.439, f32[64,8,4480]{2,1,0:T(8,128)} %get-tuple-element.422, f32[64,8]{1,0:T(8,128)S(1)} %broadcast_maximum_fusion.2, bf16[4480,2048]{1,0:T(8,128)(2,1)} %get-tuple-element.459, s32[]{:T(128)S(6)} %select_n.253), kind=kOutput, calls=%fused_computation.23.clone.1 | convolution fusion | flops 589496320 | bytes 10586628 | tf_op jit(solution)/shard_map/while/body/eval_jaxpr/cgp,pd->cgd/dot_general | solution.py:76
  535.7 1.4 fusion.100
  540.5 6.0 %fusion.99 = (f32[64,8]{1,0:T(8,128)S(1)}, f32[64,8,4480]{2,1,0:T(8,128)}) fusion(bf16[4480,2048]{1,0:T(8,128)(2,1)} %get-tuple-element.459, s32[]{:T(128)S(6)} %select_n.251, bf16[64,8,8,128]{3,2,1,0:T(8,128)(2,1)S(1)} %get-tuple-element.458, s32[]{:T(128)S(6)} %select_n.252, pred[64,4480]{1,0:T(8,128)(4,1)S(1)} %broadcast_compare_fusion.4), kind=kOutput, calls=%fused_computation.151.clone.1 | convolution fusion | flops 594083328 | bytes 10741768 | tf_op jit(solution)/shard_map/while/body/eval_jaxpr/cgd,pd->cgp/dot_general | solution.py:70
  546.5 6.1 %fusion.101 = f32[8,64,8,128]{3,2,1,0:T(8,128)} fusion(f32[8,64,8,128]{3,2,1,0:T(8,128)} %get-tuple-element.441, s32[]{:T(128)} %get-tuple-element.439, f32[64,8,4480]{2,1,0:T(8,128)} %get-tuple-element.422, f32[64,8]{1,0:T(8,128)S(1)} %broadcast_maximum_fusion.2, bf16[4480,2048]{1,0:T(8,128)(2,1)} %get-tuple-element.459, s32[]{:T(128)S(6)} %select_n.253), kind=kOutput, calls=%fused_computation.23.clone.1 | convolution fusion | flops 589496320 | bytes 10586628 | tf_op jit(solution)/shard_map/while/body/eval_jaxpr/cgp,pd->cgd/dot_general | solution.py:76
  553.2 1.4 fusion.100
  558.0 6.0 %fusion.99 = (f32[64,8]{1,0:T(8,128)S(1)}, f32[64,8,4480]{2,1,0:T(8,128)}) fusion(bf16[4480,2048]{1,0:T(8,128)(2,1)} %get-tuple-element.459, s32[]{:T(128)S(6)} %select_n.251, bf16[64,8,8,128]{3,2,1,0:T(8,128)(2,1)S(1)} %get-tuple-element.458, s32[]{:T(128)S(6)} %select_n.252, pred[64,4480]{1,0:T(8,128)(4,1)S(1)} %broadcast_compare_fusion.4), kind=kOutput, calls=%fused_computation.151.clone.1 | convolution fusion | flops 594083328 | bytes 10741768 | tf_op jit(solution)/shard_map/while/body/eval_jaxpr/cgd,pd->cgp/dot_general | solution.py:70
  564.0 6.1 %fusion.101 = f32[8,64,8,128]{3,2,1,0:T(8,128)} fusion(f32[8,64,8,128]{3,2,1,0:T(8,128)} %get-tuple-element.441, s32[]{:T(128)} %get-tuple-element.439, f32[64,8,4480]{2,1,0:T(8,128)} %get-tuple-element.422, f32[64,8]{1,0:T(8,128)S(1)} %broadcast_maximum_fusion.2, bf16[4480,2048]{1,0:T(8,128)(2,1)} %get-tuple-element.459, s32[]{:T(128)S(6)} %select_n.253), kind=kOutput, calls=%fused_computation.23.clone.1 | convolution fusion | flops 589496320 | bytes 10586628 | tf_op jit(solution)/shard_map/while/body/eval_jaxpr/cgp,pd->cgd/dot_general | solution.py:76
  570.7 1.4 fusion.100
  572.1 2.0 fusion.48
  574.3 1.3 convert_element_type.67
  (174 shorter events, 18.5 us)
Async XLA Ops:
  10.3 19.5 %all-to-all-start.1 = ((bf16[16,1,5]{2,1,0:T(2,128)(2,1)}), bf16[16,1,5]{2,1,0:T(2,128)(2,1)S(1)}, u32[]{:S(2)}, u32[]{:S(2)}) async-start(bf16[16,1,5]{2,1,0:T(2,128)(2,1)} %convert_element_type.76), calls=%async_computation.1 | async-start | bytes 16384 | tf_op jit(solution)/shard_map/all_to_all | solution.py:103
  29.7 67.4 %copy-start.1 = (bf16[1,560,2048]{2,1,0:T(8,128)(2,1)S(1)}, bf16[1,560,2048]{2,1,0:T(8,128)(2,1)}, u32[]{:S(2)}) copy-start(bf16[1,560,2048]{2,1,0:T(8,128)(2,1)} %param.15) | copy-start | bytes 6881284
  103.6 7.7 %copy-start.9 = (bf16[4,2,8192]{2,1,0:T(2,128)(2,1)S(1)}, bf16[4,2,8192]{2,1,0:T(2,128)(2,1)}, u32[]{:S(2)}) copy-start(bf16[4,2,8192]{2,1,0:T(2,128)(2,1)} %param.18) | copy-start | bytes 393220
  103.6 328.5 %all-to-all-start = ((bf16[8,1,560,2048]{3,2,1,0:T(8,128)(2,1)}), bf16[8,1,560,2048]{3,2,1,0:T(8,128)(2,1)}, u32[]{:S(2)}, u32[]{:S(2)}) async-start(bf16[8,1,560,2048]{3,2,1,0:T(8,128)(2,1)} %stack.2), calls=%async_computation | async-start | bytes 36700160 | tf_op jit(solution)/shard_map/all_to_all | solution.py:60
  111.1 314.0 %all-gather.2.cloned.1.call-start = ((), (), s32[]{:S(2)}) async-start(), calls=%async_computation.3 | async-start | bytes 2359296 | tf_op jit(solution)/shard_map/all_gather | solution.py:25
  113.3 2.0 copy-start.17
  116.6 18.6 %copy-start.13 = (s32[80]{0:T(128)}, s32[80]{0:T(128)S(1)}, u32[]{:S(2)}) copy-start(s32[80]{0:T(128)S(1)} %reshape.305) | copy-start | bytes 964
  119.3 12.0 %copy-start.15 = (pred[80]{0:T(512)(128)(4,1)}, pred[80]{0:T(512)(128)(4,1)S(1)}, u32[]{:S(2)}) copy-start(pred[80]{0:T(512)(128)(4,1)S(1)} %get-tuple-element.308) | copy-start | bytes 244
  123.1 1.7 copy-start.4
  130.0 2.4 slice-start
  130.4 1.1 copy-start.2
  130.4 2.4 slice-start.1
  135.3 1.5 copy-start.6
  135.3 1.5 copy-start.7
  135.3 3.0 copy-start.10
  135.3 4.3 copy-start.5
  136.8 5.6 copy-start.3
  136.8 5.6 copy-start.16
  142.4 5.7 copy-start.14
  427.7 2.8 copy-start.11
  427.7 4.5 copy-start.8
  427.7 4.5 copy-start.12
  441.6 6.7 %copy-start = (f32[64,8,4480]{2,1,0:T(8,128)S(1)}, f32[64,8,4480]{2,1,0:T(8,128)}, u32[]{:S(2)}) copy-start(f32[64,8,4480]{2,1,0:T(8,128)} %get-tuple-element.422) | copy-start | bytes 27525124 | tf_op jit(solution)/shard_map/while
  459.1 6.7 %copy-start = (f32[64,8,4480]{2,1,0:T(8,128)S(1)}, f32[64,8,4480]{2,1,0:T(8,128)}, u32[]{:S(2)}) copy-start(f32[64,8,4480]{2,1,0:T(8,128)} %get-tuple-element.422) | copy-start | bytes 27525124 | tf_op jit(solution)/shard_map/while
  476.6 6.7 %copy-start = (f32[64,8,4480]{2,1,0:T(8,128)S(1)}, f32[64,8,4480]{2,1,0:T(8,128)}, u32[]{:S(2)}) copy-start(f32[64,8,4480]{2,1,0:T(8,128)} %get-tuple-element.422) | copy-start | bytes 27525124 | tf_op jit(solution)/shard_map/while
  494.1 6.7 %copy-start = (f32[64,8,4480]{2,1,0:T(8,128)S(1)}, f32[64,8,4480]{2,1,0:T(8,128)}, u32[]{:S(2)}) copy-start(f32[64,8,4480]{2,1,0:T(8,128)} %get-tuple-element.422) | copy-start | bytes 27525124 | tf_op jit(solution)/shard_map/while
  511.5 6.7 %copy-start = (f32[64,8,4480]{2,1,0:T(8,128)S(1)}, f32[64,8,4480]{2,1,0:T(8,128)}, u32[]{:S(2)}) copy-start(f32[64,8,4480]{2,1,0:T(8,128)} %get-tuple-element.422) | copy-start | bytes 27525124 | tf_op jit(solution)/shard_map/while
  529.0 6.7 %copy-start = (f32[64,8,4480]{2,1,0:T(8,128)S(1)}, f32[64,8,4480]{2,1,0:T(8,128)}, u32[]{:S(2)}) copy-start(f32[64,8,4480]{2,1,0:T(8,128)} %get-tuple-element.422) | copy-start | bytes 27525124 | tf_op jit(solution)/shard_map/while
  546.5 6.7 %copy-start = (f32[64,8,4480]{2,1,0:T(8,128)S(1)}, f32[64,8,4480]{2,1,0:T(8,128)}, u32[]{:S(2)}) copy-start(f32[64,8,4480]{2,1,0:T(8,128)} %get-tuple-element.422) | copy-start | bytes 27525124 | tf_op jit(solution)/shard_map/while
  564.0 6.7 %copy-start = (f32[64,8,4480]{2,1,0:T(8,128)S(1)}, f32[64,8,4480]{2,1,0:T(8,128)}, u32[]{:S(2)}) copy-start(f32[64,8,4480]{2,1,0:T(8,128)} %get-tuple-element.422) | copy-start | bytes 27525124 | tf_op jit(solution)/shard_map/while
Sparse Core Ops, SparseCore 0:
  138.4 198.5 all-gather.1
